TPU v7x, 32 devices: a whole 2x2x4 slice. The times are simulated.
32 devices in a mesh: band: 8 (over z, core), dom: 4 (over y, x).
Axes of the slice: x: 2, y: 2, z: 4, core: 2. Of those that a mesh axis runs over, the one named last changes fastest.
Arguments:
- orbitals: bfloat16 [512, 24576], P('band', 'dom'), may hold values from -6 to 6
- rotation: bfloat16 [512, 256], P('band'), may hold values from -0.375 to 0.375
- projectors: bfloat16 [32, 16, 24576], P(None, None, 'dom'), may hold values from -0.078125 to 0.078125
- coupling: float32 [64, 16, 16], P('dom'), may hold values from -5 to 5
- slot_atom: int32 [4, 32], replicated, may hold values from 0 to 63, as said below
Outputs:
- updated_orbitals: bfloat16 [512, 24576], P('band', 'dom')
Inputs may be any that keep to these rules, and one draw needn't show every extreme that they name: `slot_atom`: the atoms of one row are distinct. Atom a is owned by domain a // 16. A row names at most 16 atoms of any one owner; domain 4 - 1 is named exactly 16 times by every row. Other owners are named between 0 and 16 times, unevenly.
All inputs are finite; a program needn't handle non-finite values.
Results may differ from a plain program's by a relative error of at most 0.0057.
Values may be sent and summed in bfloat16 or wider, within the bound.
No kernel may reach another device: no remote copies, remote signals or barrier semaphores. Data moves between devices by JAX's collectives and lax.ppermute only.
A program may use at most 64 MiB of HBM per device.

v0:
```python
import functools

import jax
import jax.numpy as jnp
from jax import lax
from jax.experimental import pallas as pl
from jax.experimental.pallas import tpu as pltpu
from jax.sharding import PartitionSpec as P

TURN = 1 * 10**9
COUPLE = 2 * 10**9
APPLY = 5 * 10**9
F32 = jnp.float32
BF16 = jnp.bfloat16
ROOM = pltpu.CompilerParams(vmem_limit_bytes=8 * 2**20)
NT = (((1,), (1,)), ((), ()))
VMEM = pl.BlockSpec(memory_space=pltpu.VMEM)
SMEM = pl.BlockSpec(memory_space=pltpu.SMEM)


def flops(count):
    return pl.CostEstimate(flops=count, bytes_accessed=0, transcendentals=0)


def call(kernel, name, outs, args, scratch=(), first=VMEM, cost=0):
    shapes = [jax.ShapeDtypeStruct(*o) for o in outs]
    return pl.pallas_call(
        kernel,
        in_specs=[first] + [VMEM] * (len(args) - 1),
        out_specs=[VMEM] * len(outs),
        out_shape=shapes,
        scratch_shapes=list(scratch),
        compiler_params=ROOM,
        cost_estimate=flops(cost),
        name=name,
    )(*args)


def along_bands(block, distance):
    count = lax.axis_size("band")
    return lax.ppermute(block, "band", [(i, (i + distance) % count) for i in range(count)])


def swapped(block):
    count = lax.axis_size("band")
    return lax.ppermute(block, "band", [(i, i ^ 1) for i in range(count)])


def on_even():
    return lax.axis_index("band") % 2 == 0


def by_permutes():
    count = lax.axis_size("dom")
    return count <= 8 and count & (count - 1) == 0


def from_all_domains(block):
    count = lax.axis_size("dom")
    if by_permutes():
        routes = [[(i, i ^ mask) for i in range(count)] for mask in range(1, count)]
        return [block] + [lax.ppermute(block, "dom", route) for route in routes]
    whole = lax.all_gather(block, "dom")
    return [whole[d] for d in range(count)]


def domain_at(place):
    return lax.axis_index("dom") ^ place if by_permutes() else place


def tile_of(extent, most):
    return max(w for w in range(128, most + 1, 128) if extent % w == 0)


def turn_kernel(coupling_ref, out_ref):
    owned, rank = coupling_ref.shape
    whole = coupling_ref[...]
    high = whole.astype(BF16)
    unit = lax.broadcasted_iota(jnp.int32, (rank, rank), 0) == lax.broadcasted_iota(
        jnp.int32, (rank, rank), 1
    )
    unit = jnp.where(unit, 1.0, 0.0).astype(BF16)
    for i, piece in enumerate((high, (whole - high.astype(F32)).astype(BF16))):
        turned = lax.dot_general(unit, piece, NT, preferred_element_type=F32)
        out_ref[:, i * owned : (i + 1) * owned] = turned.astype(BF16)


def project_kernel(orb_ref, proj_ref, turned_ref, out_ref):
    width, points = orb_ref.shape
    out_ref[width:, : turned_ref.shape[1]] = turned_ref[...]
    tile = tile_of(points, 1024)
    total = None
    for at in range(0, points, tile):
        term = lax.dot_general(
            proj_ref[:, at : at + tile], orb_ref[:, at : at + tile], NT, preferred_element_type=F32
        )
        total = term if total is None else total + term
    out_ref[:width, :] = total.T.astype(BF16)


def project(orbitals, proj, coupling):
    width, points = orbitals.shape
    owned, rank = coupling.shape
    turned = call(
        turn_kernel, "turn", [((rank, 2 * owned), BF16)], [coupling], cost=TURN
    )[0]
    outs = [((width + rank, proj.shape[0]), BF16)]
    return call(project_kernel, "project", outs, [orbitals, proj, turned])[0]


def couple_kernel(count, slots, owned, slot_ref, *refs):
    loads = refs[:count]
    out_ref, pick, high_ref, low_ref = refs[count:]
    width, flat = out_ref.shape
    rank = flat // slots
    me = lax.axis_index("dom")
    lanes = lax.broadcasted_iota(jnp.int32, (rank, flat), 1)
    unit = lanes % rank == lax.broadcasted_iota(jnp.int32, (rank, flat), 0)
    lane_slot = lanes // rank

    atoms = jnp.zeros((rank, flat), jnp.int32)
    for k in range(slots):
        atoms = jnp.where(lane_slot == k, slot_ref[me, k], atoms)

    columns = None
    for place in range(count):
        owner = domain_at(place)
        for a in range(owned):
            hit = unit & (atoms == owner * owned + a)
            pick[a * rank : (a + 1) * rank, :] = jnp.where(hit, 1.0, 0.0).astype(BF16)
        parts = [loads[place][width:, i * owned * rank : (i + 1) * owned * rank] for i in (0, 1)]
        term = jnp.dot(jnp.concatenate(parts, 0), pick[...], preferred_element_type=F32)
        columns = term if columns is None else columns + term
    high, low = columns[:rank], columns[rank:]

    total = None
    for place in range(count):
        domain = domain_at(place)
        for k in range(slots):
            hit = atoms == slot_ref[domain, k]
            rows = slice(k * rank, (k + 1) * rank)
            high_ref[rows, :] = jnp.where(hit, high, 0.0).astype(BF16)
            low_ref[rows, :] = jnp.where(hit, low, 0.0).astype(BF16)
        block = loads[place][:width, :]
        term = jnp.dot(block, high_ref[...], preferred_element_type=F32)
        term += jnp.dot(block, low_ref[...], preferred_element_type=F32)
        total = term if total is None else total + term
    out_ref[...] = total.astype(BF16)


def couple(slot_atom, loads, width, owned):
    flat = loads[0].shape[1]
    slots = slot_atom.shape[1]
    return call(
        functools.partial(couple_kernel, len(loads), slots, owned),
        "couple",
        [((width, flat), BF16)],
        [slot_atom, *loads],
        [
            pltpu.VMEM((owned * (flat // slots), flat), BF16),
            pltpu.VMEM((flat, flat), BF16),
            pltpu.VMEM((flat, flat), BF16),
        ],
        first=SMEM,
        cost=COUPLE,
    )[0]


def hold_kernel(block_ref, after_ref, out_ref):
    out_ref[...] = block_ref[...]


def hold(block, after):
    return call(hold_kernel, "hold", [(block.shape, block.dtype)], [block, after])[0]


def choose_kernel(mine, mine_two, own, two_a, two_b, coef_ref, upper_ref, lower_ref, held_ref):
    cut, half = two_a.shape[0], upper_ref.shape[0]

    @pl.when(on_even())
    def _():
        coef_ref[...] = mine[...]
        upper_ref[...] = own[:half, :]
        lower_ref[...] = own[half:, :]

    @pl.when(jnp.logical_not(on_even()))
    def _():
        coef_ref[...] = mine_two[...]
        upper_ref[...] = two_a[:half, :]
        lower_ref[: cut - half, :] = two_a[half:, :]
        lower_ref[cut - half :, :] = two_b[...]

    held_ref[...] = two_b[...]


def choose(mine, mine_two, own, two_a, two_b):
    args = [mine, mine_two, own, two_a, two_b]
    half = ((own.shape[0] // 2, own.shape[1]), own.dtype)
    outs = [(mine.shape, mine.dtype), half, half, (two_b.shape, two_b.dtype)]
    return call(choose_kernel, "choose", outs, args)


def apply_kernel(rot_ref, mine, one, two, three, proj_ref, out_ref):
    width, flat = mine.shape
    points = proj_ref.shape[1]
    mixed = None
    blocks = [mine, one, two, three]
    for s, block in enumerate(blocks):
        term = jnp.dot(
            rot_ref[:, s * width : (s + 1) * width], block[...], preferred_element_type=F32
        )
        mixed = term if mixed is None else mixed + term
    mixed = mixed.astype(BF16)
    tile = tile_of(points, 1024)
    for at in range(0, points, tile):
        out_ref[:, at : at + tile] = jnp.dot(
            mixed, proj_ref[:, at : at + tile], preferred_element_type=F32
        )


def gather_kernel(rot_ref, own, one_a, two_a, two_b, three_a, out_ref, stack):
    width, points = own.shape
    first, second = width + one_a.shape[0], 2 * width
    turn = jnp.concatenate(
        [rot_ref[:, :first], rot_ref[:, second : second + stack.shape[0] - first]], axis=1
    )
    tile = tile_of(points, 1024)
    for i in range(points // tile):
        here = slice(i * tile, (i + 1) * tile)
        at = 0
        for ref in (own, one_a, two_a, two_b, three_a):
            stack[at : at + ref.shape[0], here] = ref[:, here]
            at += ref.shape[0]
        out_ref[:, here] = jnp.dot(turn, stack[:, here], preferred_element_type=F32)


def gather(rotation, *blocks):
    width, points = blocks[0].shape
    depth = sum(block.shape[0] for block in blocks)
    scratch = [pltpu.VMEM((depth, points), BF16)]
    return call(
        gather_kernel, "gather", [((width, points), F32)], [rotation, *blocks], scratch
    )[0]


def finish_kernel(rot_ref, partial_ref, one_b, three_b, applied, out_hbm, out_ref, sems):
    width, points = out_ref.shape
    pieces = sems.shape[0]
    tile = points // pieces
    turn = jnp.concatenate(
        [
            rot_ref[:, 2 * width - one_b.shape[0] : 2 * width],
            rot_ref[:, 4 * width - three_b.shape[0] :],
        ],
        axis=1,
    )
    copies = []
    for i in range(pieces):
        here = slice(i * tile, (i + 1) * tile)
        last = jnp.concatenate([one_b[:, here], three_b[:, here]], axis=0)
        rotated = partial_ref[:, here] + jnp.dot(turn, last, preferred_element_type=F32)
        added = rotated.astype(BF16).astype(F32) + applied[:, here]
        out_ref[:, here] = added.astype(out_ref.dtype)
        part = (slice(None), pl.ds(i * tile, tile))
        copies.append(pltpu.make_async_copy(out_ref.at[part], out_hbm.at[part], sems.at[i]))
        copies[-1].start()
    for copy in copies:
        copy.wait()


def finish(*args):
    width, points = args[-1].shape
    pieces = points // tile_of(points, 1024)
    return pl.pallas_call(
        finish_kernel,
        in_specs=[VMEM] * len(args),
        out_specs=pl.BlockSpec(memory_space=pl.ANY),
        out_shape=jax.ShapeDtypeStruct((width, points), BF16),
        scratch_shapes=[pltpu.VMEM((width, points), BF16), pltpu.SemaphoreType.DMA((pieces,))],
        compiler_params=ROOM,
        cost_estimate=flops(0),
        name="finish",
    )(*args)


def on_device(orbitals, rotation, projectors, coupling, slot_atom):
    width, points = orbitals.shape
    slot_count, rank, _ = projectors.shape
    owned = coupling.shape[0]
    proj = projectors.reshape(slot_count * rank, points)

    cut = width * 3 // 4
    two_a = along_bands(orbitals[:cut], 2)
    two_b = along_bands(orbitals[cut:], 2)
    loads = from_all_domains(project(orbitals, proj, coupling.reshape(owned * rank, rank)))
    mine = couple(slot_atom, loads, width, owned)
    mine_two = along_bands(mine, 2)
    three_a = along_bands(hold(two_a, mine), 1)
    other, upper, lower, held = choose(mine, mine_two, orbitals, two_a, two_b)
    mine_three = along_bands(mine_two, 1)
    mine_one = swapped(other)
    three_b = along_bands(held, 1)
    one_a, one_b = swapped(upper), swapped(lower)
    applied = call(
        apply_kernel,
        "apply",
        [((width, points), F32)],
        [rotation, mine, mine_one, mine_two, mine_three, proj],
        cost=APPLY,
    )[0]
    partial = gather(rotation, orbitals, one_a, two_a, two_b, three_a)
    return finish(rotation, partial, one_b, three_b, applied)


def solution(mesh):
    in_specs = (P("band", "dom"), P("band", None), P(None, None, "dom"), P("dom", None, None), P())
    out_specs = P("band", "dom")
    return jax.shard_map(
        on_device, mesh=mesh, in_specs=in_specs, out_specs=out_specs, check_vma=False
    )
```

profile of v0, /device:TPU:0, one launch (start us, length us, event | category | flops | bytes accessed | tf_op | source)
XLA Modules:
  0.0 36.7 jit_solution(5760476306702142822)
XLA Ops:
  0.0 1.1 %slice.6 = bf16[48,6144]{1,0:T(8,128)(2,1)S(1)} slice(bf16[64,6144]{1,0:T(8,128)(2,1)} %own.3), slice={[0:48], [0:6144]} | slice | bytes 1179648 | tf_op jit(solution)/shard_map/slice | solution.py:293
  1.1 3.1 %collective-permute-start.4 = (bf16[48,6144]{1,0:T(8,128)(2,1)S(1)}, bf16[48,6144]{1,0:T(8,128)(2,1)S(1)}, u32[]{:S(2)}, u32[]{:S(2)}) collective-permute-start(bf16[48,6144]{1,0:T(8,128)(2,1)S(1)} %slice.6), channel_id=1, source_target_pairs={{0,8},{4,12},{8,16},{12,20},{16,24},{20,28},{24,0},{28,4},{1,9},{5... | collective-permute-start | bytes 1769480 | tf_op jit(solution)/shard_map/ppermute | solution.py:41
  4.2 0.0 copy-start.3
  4.2 0.9 %copy-done.3 = f32[16,16,16]{2,1,0:T(8,128)S(1)} copy-done((f32[16,16,16]{2,1,0:T(8,128)S(1)}, f32[16,16,16]{2,1,0:T(8,128)}, u32[]{:S(2)}) %copy-start.3) | copy-done | bytes 16408
  5.1 0.0 copy-start
  5.1 0.1 turn.1.turned_ref
  5.2 1.0 %copy-done = bf16[64,6144]{1,0:T(8,128)(2,1)S(1)} copy-done((bf16[64,6144]{1,0:T(8,128)(2,1)S(1)}, bf16[64,6144]{1,0:T(8,128)(2,1)}, u32[]{:S(2)}) %copy-start) | copy-done | bytes 786456
  6.2 0.0 copy-start.1
  6.2 2.8 %copy-done.1 = bf16[32,16,6144]{2,1,0:T(8,128)(2,1)S(1)} copy-done((bf16[32,16,6144]{2,1,0:T(8,128)(2,1)S(1)}, bf16[32,16,6144]{2,1,0:T(8,128)(2,1)}, u32[]{:S(2)}) %copy-start.1) | copy-done | bytes 6291480
  9.0 0.0 copy-start.4
  9.0 0.0 slice-start
  9.0 1.8 %project.1.refs_0_ = bf16[80,512]{1,0:T(8,128)(2,1)S(1)} custom-call(bf16[64,6144]{1,0:T(8,128)(2,1)S(1)} %copy-done, bf16[512,6144]{1,0:T(8,128)(2,1)S(1)} %bitcast.2, bf16[16,512]{1,0:T(8,128)(2,1)S(1)} %turn.1.turned_ref), custom_call_target="tpu_custom_call" | custom-call | tf_op jit(solution)/shard_map/project/pallas_call | solution.py:27
  10.8 2.5 %collective-permute-start.2 = (bf16[80,512]{1,0:T(8,128)(2,1)S(1)}, bf16[80,512]{1,0:T(8,128)(2,1)S(1)}, u32[]{:S(2)}, u32[]{:S(2)}) collective-permute-start(bf16[80,512]{1,0:T(8,128)(2,1)S(1)} %project.1.refs_0_), channel_id=1, source_target_pairs={{0,3},{1,2},{2,1},{3,0},{4,7},{5,6},{6,5},{7,4},{8,11},{9,10},{10,... | collective-permute-start | bytes 245768 | tf_op jit(solution)/shard_map/ppermute | solution.py:62
  13.4 0.5 %collective-permute-start.1 = (bf16[80,512]{1,0:T(8,128)(2,1)S(1)}, bf16[80,512]{1,0:T(8,128)(2,1)S(1)}, u32[]{:S(2)}, u32[]{:S(2)}) collective-permute-start(bf16[80,512]{1,0:T(8,128)(2,1)S(1)} %project.1.refs_0_), channel_id=1, source_target_pairs={{0,2},{1,3},{2,0},{3,1},{4,6},{5,7},{6,4},{7,5},{8,10},{9,11},{10,... | collective-permute-start | bytes 245768 | tf_op jit(solution)/shard_map/ppermute | solution.py:62
  13.9 0.5 %collective-permute-start = (bf16[80,512]{1,0:T(8,128)(2,1)S(1)}, bf16[80,512]{1,0:T(8,128)(2,1)S(1)}, u32[]{:S(2)}, u32[]{:S(2)}) collective-permute-start(bf16[80,512]{1,0:T(8,128)(2,1)S(1)} %project.1.refs_0_), channel_id=1, source_target_pairs={{0,1},{1,0},{2,3},{3,2},{4,5},{5,4},{6,7},{7,6},{8,9},{9,8},{10,11... | collective-permute-start | bytes 245768 | tf_op jit(solution)/shard_map/ppermute | solution.py:62
  14.4 0.0 slice-start.1
  14.4 1.6 %collective-permute-start.5 = (bf16[16,6144]{1,0:T(8,128)(2,1)S(1)}, bf16[16,6144]{1,0:T(8,128)(2,1)S(1)}, u32[]{:S(2)}, u32[]{:S(2)}) collective-permute-start(bf16[16,6144]{1,0:T(8,128)(2,1)S(1)} %slice.7), channel_id=1, source_target_pairs={{0,8},{4,12},{8,16},{12,20},{16,24},{20,28},{24,0},{28,4},{1,9},{5... | collective-permute-start | bytes 589832 | tf_op jit(solution)/shard_map/ppermute | solution.py:41
  16.1 0.3 collective-permute-done.2.refs_3_
  16.4 1.5 %collective-permute-done.1.refs_2_ = bf16[80,512]{1,0:T(8,128)(2,1)S(1)} collective-permute-done((bf16[80,512]{1,0:T(8,128)(2,1)S(1)}, bf16[80,512]{1,0:T(8,128)(2,1)S(1)}, u32[]{:S(2)}, u32[]{:S(2)}) %collective-permute-start.1) | collective-permute-done | bytes 81952 | tf_op jit(solution)/shard_map/ppermute | solution.py:62
  17.9 0.4 %collective-permute-done.refs_1_ = bf16[80,512]{1,0:T(8,128)(2,1)S(1)} collective-permute-done((bf16[80,512]{1,0:T(8,128)(2,1)S(1)}, bf16[80,512]{1,0:T(8,128)(2,1)S(1)}, u32[]{:S(2)}, u32[]{:S(2)}) %collective-permute-start) | collective-permute-done | bytes 81952 | tf_op jit(solution)/shard_map/ppermute | solution.py:62
  18.3 0.0 copy-done.4
  18.3 1.5 %couple.1.mine.after_ref = bf16[64,512]{1,0:T(8,128)(2,1)S(1)} custom-call(s32[4,32]{1,0:T(4,128)S(1)} %copy-done.4, bf16[80,512]{1,0:T(8,128)(2,1)S(1)} %project.1.refs_0_, bf16[80,512]{1,0:T(8,128)(2,1)S(1)} %collective-permute-done.refs_1_, bf16[80,512]{1,0:T(8,128)(2,1)S(1)} %collective-permute-done.1.refs_2_, ...), custom_call_target="tpu_custom_call" | custom-call | flops 2000000000 | tf_op jit(solution)/shard_map/couple/pallas_call | solution.py:27
  19.8 0.0 copy-start.2
  19.9 1.6 %collective-permute-start.3 = (bf16[64,512]{1,0:T(8,128)(2,1)S(1)}, bf16[64,512]{1,0:T(8,128)(2,1)S(1)}, u32[]{:S(2)}, u32[]{:S(2)}) collective-permute-start(bf16[64,512]{1,0:T(8,128)(2,1)S(1)} %couple.1.mine.after_ref), channel_id=1, source_target_pairs={{0,8},{4,12},{8,16},{12,20},{16,24},{20,28},{24,0},{28,4},{1,9},{5... | collective-permute-start | bytes 196616 | tf_op jit(solution)/shard_map/ppermute | solution.py:41
  21.5 0.0 collective-permute-done.4.two_a.block_ref
  21.5 0.1 collective-permute-start.7
  21.6 4.4 %collective-permute-done.3.mine_two.two = bf16[64,512]{1,0:T(8,128)(2,1)S(1)} collective-permute-done((bf16[64,512]{1,0:T(8,128)(2,1)S(1)}, bf16[64,512]{1,0:T(8,128)(2,1)S(1)}, u32[]{:S(2)}, u32[]{:S(2)}) %collective-permute-start.3) | collective-permute-done | bytes 65568 | tf_op jit(solution)/shard_map/ppermute | solution.py:41
  26.0 0.0 collective-permute-start.11
  26.0 0.0 collective-permute-done.5.two_b
  26.0 0.1 choose.1
  26.1 0.1 collective-permute-start.10
  26.1 0.5 %collective-permute-start.9 = (bf16[16,6144]{1,0:T(8,128)(2,1)S(1)}, bf16[16,6144]{1,0:T(8,128)(2,1)S(1)}, u32[]{:S(2)}, u32[]{:S(2)}) collective-permute-start(bf16[16,6144]{1,0:T(8,128)(2,1)S(1)} %get-tuple-element.11), channel_id=1, source_target_pairs={{0,4},{4,8},{8,12},{12,16},{16,20},{20,24},{24,28},{28,0},{1,5},{5... | collective-permute-start | bytes 589832 | tf_op jit(solution)/shard_map/ppermute | solution.py:41
  26.6 1.8 %collective-permute-start.6 = (bf16[32,6144]{1,0:T(8,128)(2,1)S(1)}, bf16[32,6144]{1,0:T(8,128)(2,1)S(1)}, u32[]{:S(2)}, u32[]{:S(2)}) collective-permute-start(bf16[32,6144]{1,0:T(8,128)(2,1)S(1)} %get-tuple-element.9), channel_id=1, source_target_pairs={{0,4},{4,0},{8,12},{12,8},{16,20},{20,16},{24,28},{28,24},{1,5},{5... | collective-permute-start | bytes 1179656 | tf_op jit(solution)/shard_map/ppermute | solution.py:46
  28.4 5.0 %collective-permute-done.11.three = bf16[64,512]{1,0:T(8,128)(2,1)S(1)} collective-permute-done((bf16[64,512]{1,0:T(8,128)(2,1)S(1)}, bf16[64,512]{1,0:T(8,128)(2,1)S(1)}, u32[]{:S(2)}, u32[]{:S(2)}) %collective-permute-start.11) | collective-permute-done | bytes 65568 | tf_op jit(solution)/shard_map/ppermute | solution.py:41
  33.4 0.0 collective-permute-start.8
  33.4 0.0 collective-permute-done.10.one
  33.4 0.0 slice-done
  33.4 0.0 slice-done.1
  33.4 0.0 copy-done.2
  33.4 1.4 %apply.1.applied = f32[64,6144]{1,0:T(8,128)S(1)} custom-call(bf16[64,256]{1,0:T(8,128)(2,1)S(1)} %copy-done.2, bf16[64,512]{1,0:T(8,128)(2,1)S(1)} %couple.1.mine.after_ref, bf16[64,512]{1,0:T(8,128)(2,1)S(1)} %collective-permute-done.10.one, bf16[64,512]{1,0:T(8,128)(2,1)S(1)} %collective-permute-done.3.mine_two.two, ...), custom_call_target="tpu_custom_call" | custom-call | flops 5000000000 | tf_op jit(solution)/shard_map/apply/pallas_call | solution.py:27
  34.9 0.0 collective-permute-done.6.one_a
  34.9 0.0 collective-permute-done.7.three_a
  34.9 0.6 %gather.1.partial_ref = f32[64,6144]{1,0:T(8,128)S(1)} custom-call(bf16[64,256]{1,0:T(8,128)(2,1)S(1)} %copy-done.2, bf16[64,6144]{1,0:T(8,128)(2,1)S(1)} %copy-done, bf16[32,6144]{1,0:T(8,128)(2,1)S(1)} %collective-permute-done.6.one_a, bf16[48,6144]{1,0:T(8,128)(2,1)S(1)} %collective-permute-done.4.two_a.block_ref, ...), custom_call_target="tpu_custom_call" | custom-call | tf_op jit(solution)/shard_map/gather/pallas_call | solution.py:27
  35.5 0.0 collective-permute-done.9.three_b
  35.5 0.0 collective-permute-done.8.one_b
  35.5 1.2 %finish.1 = bf16[64,6144]{1,0:T(8,128)(2,1)} custom-call(bf16[64,256]{1,0:T(8,128)(2,1)S(1)} %copy-done.2, f32[64,6144]{1,0:T(8,128)S(1)} %gather.1.partial_ref, bf16[32,6144]{1,0:T(8,128)(2,1)S(1)} %collective-permute-done.8.one_b, bf16[16,6144]{1,0:T(8,128)(2,1)S(1)} %collective-permute-done.9.three_b, f32[64,6144]{1,0:T(8,128)S(1)} %apply.1.applied), custom_call_target="tpu_custom_call" | custom-call | tf_op jit(solution)/shard_map/finish/pallas_call | solution.py:274
  (3 shorter events, 0.1 us)
Async XLA Ops:
  1.1 20.4 %collective-permute-start.4 = (bf16[48,6144]{1,0:T(8,128)(2,1)S(1)}, bf16[48,6144]{1,0:T(8,128)(2,1)S(1)}, u32[]{:S(2)}, u32[]{:S(2)}) collective-permute-start(bf16[48,6144]{1,0:T(8,128)(2,1)S(1)} %slice.6), channel_id=1, source_target_pairs={{0,8},{4,12},{8,16},{12,20},{16,24},{20,28},{24,0},{28,4},{1,9},{5... | collective-permute-start | bytes 1769480 | tf_op jit(solution)/shard_map/ppermute | solution.py:41
  4.2 0.9 %copy-start.3 = (f32[16,16,16]{2,1,0:T(8,128)S(1)}, f32[16,16,16]{2,1,0:T(8,128)}, u32[]{:S(2)}) copy-start(f32[16,16,16]{2,1,0:T(8,128)} %param.8) | copy-start | bytes 49156
  5.1 1.1 %copy-start = (bf16[64,6144]{1,0:T(8,128)(2,1)S(1)}, bf16[64,6144]{1,0:T(8,128)(2,1)}, u32[]{:S(2)}) copy-start(bf16[64,6144]{1,0:T(8,128)(2,1)} %own.3) | copy-start | bytes 2359300
  6.2 2.8 %copy-start.1 = (bf16[32,16,6144]{2,1,0:T(8,128)(2,1)S(1)}, bf16[32,16,6144]{2,1,0:T(8,128)(2,1)}, u32[]{:S(2)}) copy-start(bf16[32,16,6144]{2,1,0:T(8,128)(2,1)} %param.7) | copy-start | bytes 18874372
  9.0 9.3 %copy-start.4 = (s32[4,32]{1,0:T(4,128)S(1)}, s32[4,32]{1,0:T(4,128)}, u32[]{:S(2)}) copy-start(s32[4,32]{1,0:T(4,128)} %slot_ref.1) | copy-start | bytes 1540
  9.0 24.4 %slice-start = ((s8[6291456]{0:T(1024)(128)(4,1)}), s8[4194304]{0:T(1024)(128)(4,1)S(1)}, s32[]{:S(2)}) async-start(s8[6291456]{0:T(1024)(128)(4,1)} %bitcast.3), calls=%async_computation | async-start | bytes 8388608
  10.8 5.5 %collective-permute-start.2 = (bf16[80,512]{1,0:T(8,128)(2,1)S(1)}, bf16[80,512]{1,0:T(8,128)(2,1)S(1)}, u32[]{:S(2)}, u32[]{:S(2)}) collective-permute-start(bf16[80,512]{1,0:T(8,128)(2,1)S(1)} %project.1.refs_0_), channel_id=1, source_target_pairs={{0,3},{1,2},{2,1},{3,0},{4,7},{5,6},{6,5},{7,4},{8,11},{9,10},{10,... | collective-permute-start | bytes 245768 | tf_op jit(solution)/shard_map/ppermute | solution.py:62
  13.4 4.5 %collective-permute-start.1 = (bf16[80,512]{1,0:T(8,128)(2,1)S(1)}, bf16[80,512]{1,0:T(8,128)(2,1)S(1)}, u32[]{:S(2)}, u32[]{:S(2)}) collective-permute-start(bf16[80,512]{1,0:T(8,128)(2,1)S(1)} %project.1.refs_0_), channel_id=1, source_target_pairs={{0,2},{1,3},{2,0},{3,1},{4,6},{5,7},{6,4},{7,5},{8,10},{9,11},{10,... | collective-permute-start | bytes 245768 | tf_op jit(solution)/shard_map/ppermute | solution.py:62
  13.9 4.4 %collective-permute-start = (bf16[80,512]{1,0:T(8,128)(2,1)S(1)}, bf16[80,512]{1,0:T(8,128)(2,1)S(1)}, u32[]{:S(2)}, u32[]{:S(2)}) collective-permute-start(bf16[80,512]{1,0:T(8,128)(2,1)S(1)} %project.1.refs_0_), channel_id=1, source_target_pairs={{0,1},{1,0},{2,3},{3,2},{4,5},{5,4},{6,7},{7,6},{8,9},{9,8},{10,11... | collective-permute-start | bytes 245768 | tf_op jit(solution)/shard_map/ppermute | solution.py:62
  14.4 19.0 %slice-start.1 = ((s8[6291456]{0:T(1024)(128)(4,1)}), s8[2097152]{0:T(1024)(128)(4,1)S(1)}, s32[]{:S(2)}) async-start(s8[6291456]{0:T(1024)(128)(4,1)} %bitcast.3), calls=%async_computation.1 | async-start | bytes 4194304
  14.4 11.5 %collective-permute-start.5 = (bf16[16,6144]{1,0:T(8,128)(2,1)S(1)}, bf16[16,6144]{1,0:T(8,128)(2,1)S(1)}, u32[]{:S(2)}, u32[]{:S(2)}) collective-permute-start(bf16[16,6144]{1,0:T(8,128)(2,1)S(1)} %slice.7), channel_id=1, source_target_pairs={{0,8},{4,12},{8,16},{12,20},{16,24},{20,28},{24,0},{28,4},{1,9},{5... | collective-permute-start | bytes 589832 | tf_op jit(solution)/shard_map/ppermute | solution.py:41
  19.8 13.6 %copy-start.2 = (bf16[64,256]{1,0:T(8,128)(2,1)S(1)}, bf16[64,256]{1,0:T(8,128)(2,1)}, u32[]{:S(2)}) copy-start(bf16[64,256]{1,0:T(8,128)(2,1)} %rot_ref.5) | copy-start | bytes 98308
  19.9 6.1 %collective-permute-start.3 = (bf16[64,512]{1,0:T(8,128)(2,1)S(1)}, bf16[64,512]{1,0:T(8,128)(2,1)S(1)}, u32[]{:S(2)}, u32[]{:S(2)}) collective-permute-start(bf16[64,512]{1,0:T(8,128)(2,1)S(1)} %couple.1.mine.after_ref), channel_id=1, source_target_pairs={{0,8},{4,12},{8,16},{12,20},{16,24},{20,28},{24,0},{28,4},{1,9},{5... | collective-permute-start | bytes 196616 | tf_op jit(solution)/shard_map/ppermute | solution.py:41
  21.5 13.4 %collective-permute-start.7 = (bf16[48,6144]{1,0:T(8,128)(2,1)S(1)}, bf16[48,6144]{1,0:T(8,128)(2,1)S(1)}, u32[]{:S(2)}, u32[]{:S(2)}) collective-permute-start(bf16[48,6144]{1,0:T(8,128)(2,1)S(1)} %hold.1), channel_id=1, source_target_pairs={{0,4},{4,8},{8,12},{12,16},{16,20},{20,24},{24,28},{28,0},{1,5},{5... | collective-permute-start | bytes 1769480 | tf_op jit(solution)/shard_map/ppermute | solution.py:41
  26.0 7.4 %collective-permute-start.11 = (bf16[64,512]{1,0:T(8,128)(2,1)S(1)}, bf16[64,512]{1,0:T(8,128)(2,1)S(1)}, u32[]{:S(2)}, u32[]{:S(2)}) collective-permute-start(bf16[64,512]{1,0:T(8,128)(2,1)S(1)} %collective-permute-done.3.mine_two.two), channel_id=1, source_target_pairs={{0,4},{4,8},{8,12},{12,16},{16,20},{20,24},{24,28},{28,0},{1,5},{5... | collective-permute-start | bytes 196616 | tf_op jit(solution)/shard_map/ppermute | solution.py:41
  26.1 7.3 %collective-permute-start.10 = (bf16[64,512]{1,0:T(8,128)(2,1)S(1)}, bf16[64,512]{1,0:T(8,128)(2,1)S(1)}, u32[]{:S(2)}, u32[]{:S(2)}) collective-permute-start(bf16[64,512]{1,0:T(8,128)(2,1)S(1)} %get-tuple-element.12), channel_id=1, source_target_pairs={{0,4},{4,0},{8,12},{12,8},{16,20},{20,16},{24,28},{28,24},{1,5},{5... | collective-permute-start | bytes 196616 | tf_op jit(solution)/shard_map/ppermute | solution.py:46
  26.1 9.4 %collective-permute-start.9 = (bf16[16,6144]{1,0:T(8,128)(2,1)S(1)}, bf16[16,6144]{1,0:T(8,128)(2,1)S(1)}, u32[]{:S(2)}, u32[]{:S(2)}) collective-permute-start(bf16[16,6144]{1,0:T(8,128)(2,1)S(1)} %get-tuple-element.11), channel_id=1, source_target_pairs={{0,4},{4,8},{8,12},{12,16},{16,20},{20,24},{24,28},{28,0},{1,5},{5... | collective-permute-start | bytes 589832 | tf_op jit(solution)/shard_map/ppermute | solution.py:41
  26.6 8.2 %collective-permute-start.6 = (bf16[32,6144]{1,0:T(8,128)(2,1)S(1)}, bf16[32,6144]{1,0:T(8,128)(2,1)S(1)}, u32[]{:S(2)}, u32[]{:S(2)}) collective-permute-start(bf16[32,6144]{1,0:T(8,128)(2,1)S(1)} %get-tuple-element.9), channel_id=1, source_target_pairs={{0,4},{4,0},{8,12},{12,8},{16,20},{20,16},{24,28},{28,24},{1,5},{5... | collective-permute-start | bytes 1179656 | tf_op jit(solution)/shard_map/ppermute | solution.py:46
  33.4 2.1 %collective-permute-start.8 = (bf16[32,6144]{1,0:T(8,128)(2,1)S(1)}, bf16[32,6144]{1,0:T(8,128)(2,1)S(1)}, u32[]{:S(2)}, u32[]{:S(2)}) collective-permute-start(bf16[32,6144]{1,0:T(8,128)(2,1)S(1)} %get-tuple-element.10), channel_id=1, source_target_pairs={{0,4},{4,0},{8,12},{12,8},{16,20},{20,16},{24,28},{28,24},{1,5},{5... | collective-permute-start | bytes 1179656 | tf_op jit(solution)/shard_map/ppermute | solution.py:46
where the time goes:
time: 37 us; the launch traced here: 36.7 us
  starting transfers between devices  12.3 us (33%)
  waiting for transfers between devices  11.6 us (31%)
  Pallas kernels  6.83 us (18%)
  local copies, waits for them, and re-layouts  5.81 us (16%)
    ppermute x6, waiting for transfers between devices, along_bands(): lax.ppermute(block, 'band', [(i, (i + distance) % count) for i in range(c...  9.37 us
    ppermute x6, starting transfers between devices, along_bands(): lax.ppermute(block, 'band', [(i, (i + distance) % count) for i in range(c...  6.89 us
    pallas_call x7, Pallas kernels, call(): pl.pallas_call(kernel, in_specs=[first] + [VMEM] * (len(args) - 1), out_s...  5.66 us
    unnamed x14, local copies, waits for them, and re-layouts  4.7 us
    ppermute x3, starting transfers between devices, from_all_domains(): return [block] + [lax.ppermute(block, 'dom', route) for route in routes]  3.55 us
    ppermute x3, waiting for transfers between devices, from_all_domains(): return [block] + [lax.ppermute(block, 'dom', route) for route in routes]  2.24 us
    ppermute x3, starting transfers between devices, swapped(): return lax.ppermute(block, 'band', [(i, i ^ 1) for i in range(count)])  1.84 us
    pallas_call x1, Pallas kernels, finish(): pl.pallas_call(finish_kernel, in_specs=[VMEM] * len(args), out_specs=pl.B...  1.16 us
  transfers between devices with their start and end apart: 12, of which 5 were waited for; matrix products, arithmetic and copies ran while one was open for 0% of the time, Pallas kernels for 15%

commit v1 on v0

--- a/solution.py
+++ b/solution.py
@@ -7,9 +7,10 @@
 from jax.experimental.pallas import tpu as pltpu
 from jax.sharding import PartitionSpec as P
 
-TURN = 1 * 10**9
+TURN = 3 * 10**9
 COUPLE = 2 * 10**9
-APPLY = 5 * 10**9
+APPLY = 60 * 10**8
+SELECT = 20 * 10**8
 F32 = jnp.float32
 BF16 = jnp.bfloat16
 ROOM = pltpu.CompilerParams(vmem_limit_bytes=8 * 2**20)
@@ -109,8 +110,9 @@
 
 
 def couple_kernel(count, slots, owned, slot_ref, *refs):
-    loads = refs[:count]
-    out_ref, pick, high_ref, low_ref = refs[count:]
+    loads, pass_ref = refs[:count], refs[count]
+    out_ref, passed_ref, pick, high_ref, low_ref = refs[count + 1 :]
+    passed_ref[...] = pass_ref[...]
     width, flat = out_ref.shape
     rank = flat // slots
     me = lax.axis_index("dom")
@@ -148,14 +150,14 @@
     out_ref[...] = total.astype(BF16)
 
 
-def couple(slot_atom, loads, width, owned):
+def couple(slot_atom, loads, width, owned, passed):
     flat = loads[0].shape[1]
     slots = slot_atom.shape[1]
     return call(
         functools.partial(couple_kernel, len(loads), slots, owned),
         "couple",
-        [((width, flat), BF16)],
-        [slot_atom, *loads],
+        [((width, flat), BF16), (passed.shape, passed.dtype)],
+        [slot_atom, *loads, passed],
         [
             pltpu.VMEM((owned * (flat // slots), flat), BF16),
             pltpu.VMEM((flat, flat), BF16),
@@ -163,7 +165,7 @@
         ],
         first=SMEM,
         cost=COUPLE,
-    )[0]
+    )
 
 
 def hold_kernel(block_ref, after_ref, out_ref):
@@ -174,18 +176,33 @@
     return call(hold_kernel, "hold", [(block.shape, block.dtype)], [block, after])[0]
 
 
-def choose_kernel(mine, mine_two, own, two_a, two_b, coef_ref, upper_ref, lower_ref, held_ref):
-    cut, half = two_a.shape[0], upper_ref.shape[0]
+def select_kernel(even_ref, odd_ref, out_ref, odd_again_ref):
+    odd_again_ref[...] = odd_ref[...]
 
     @pl.when(on_even())
     def _():
-        coef_ref[...] = mine[...]
+        out_ref[...] = even_ref[...]
+
+    @pl.when(jnp.logical_not(on_even()))
+    def _():
+        out_ref[...] = odd_ref[...]
+
+
+def select(for_even, for_odd):
+    outs = [(for_even.shape, for_even.dtype)] * 2
+    return call(select_kernel, "select", outs, [for_even, for_odd], cost=SELECT)
+
+
+def choose_kernel(own, two_a, two_b, after_ref, upper_ref, lower_ref, held_ref):
+    cut, half = two_a.shape[0], upper_ref.shape[0]
+
+    @pl.when(on_even())
+    def _():
         upper_ref[...] = own[:half, :]
         lower_ref[...] = own[half:, :]
 
     @pl.when(jnp.logical_not(on_even()))
     def _():
-        coef_ref[...] = mine_two[...]
         upper_ref[...] = two_a[:half, :]
         lower_ref[: cut - half, :] = two_a[half:, :]
         lower_ref[cut - half :, :] = two_b[...]
@@ -193,11 +210,10 @@
     held_ref[...] = two_b[...]
 
 
-def choose(mine, mine_two, own, two_a, two_b):
-    args = [mine, mine_two, own, two_a, two_b]
+def choose(own, two_a, two_b, after):
     half = ((own.shape[0] // 2, own.shape[1]), own.dtype)
-    outs = [(mine.shape, mine.dtype), half, half, (two_b.shape, two_b.dtype)]
-    return call(choose_kernel, "choose", outs, args)
+    outs = [half, half, (two_b.shape, two_b.dtype)]
+    return call(choose_kernel, "choose", outs, [own, two_a, two_b, after])
 
 
 def apply_kernel(rot_ref, mine, one, two, three, proj_ref, out_ref):
@@ -291,14 +307,15 @@
 
     cut = width * 3 // 4
     two_a = along_bands(orbitals[:cut], 2)
-    two_b = along_bands(orbitals[cut:], 2)
     loads = from_all_domains(project(orbitals, proj, coupling.reshape(owned * rank, rank)))
-    mine = couple(slot_atom, loads, width, owned)
+    mine, own_b = couple(slot_atom, loads, width, owned, orbitals[cut:])
     mine_two = along_bands(mine, 2)
-    three_a = along_bands(hold(two_a, mine), 1)
-    other, upper, lower, held = choose(mine, mine_two, orbitals, two_a, two_b)
+    two_b = along_bands(own_b, 2)
+    other, mine_two = select(mine, mine_two)
     mine_three = along_bands(mine_two, 1)
     mine_one = swapped(other)
+    three_a = along_bands(hold(two_a, other), 1)
+    upper, lower, held = choose(orbitals, two_a, two_b, other)
     three_b = along_bands(held, 1)
     one_a, one_b = swapped(upper), swapped(lower)
     applied = call(

time: 37 us -> 40 us (1.081)
  waiting for transfers between devices: 11.6 us -> 18.4 us
  local copies, waits for them, and re-layouts: 5.81 us -> 3.88 us
  starting transfers between devices: 12.3 us -> 10.6 us
    ppermute x6, waiting for transfers between devices: 9.37 us -> 14.5 us  [along_bands(): lax.ppermute(block, 'band', [(i, (i + distance) % count) for i in range(c...]
    unnamed x14 -> x12, local copies, waits for them, and re-layouts: 4.7 us -> 2.61 us
    ppermute x3, starting transfers between devices: 1.84 us -> 0.14 us  [swapped(): return lax.ppermute(block, 'band', [(i, i ^ 1) for i in range(count)])]
    ppermute x3, waiting for transfers between devices: 2.24 us -> 3.89 us  [from_all_domains(): return [block] + [lax.ppermute(block, 'dom', route) for route in routes]]
    pallas_call x7 -> x8, Pallas kernels: 5.66 us -> 5.67 us  [call(): pl.pallas_call(kernel, in_specs=[first] + [VMEM] * (len(args) - 1), out_s...]
  transfers between devices with their start and end apart: 12 -> 12, of which waited for: 5 -> 8; matrix products, arithmetic and copies ran while one was open for 0% -> 0% of each run, Pallas kernels for 15% -> 14%
where the time goes in v1:
time: 40 us; the launch traced here: 39.9 us
  waiting for transfers between devices  18.4 us (46%)
  starting transfers between devices  10.6 us (26%)
  Pallas kernels  6.84 us (17%)
  local copies, waits for them, and re-layouts  3.88 us (10%)
    ppermute x6, waiting for transfers between devices, along_bands(): lax.ppermute(block, 'band', [(i, (i + distance) % count) for i in range(c...  14.5 us
    ppermute x6, starting transfers between devices, along_bands(): lax.ppermute(block, 'band', [(i, (i + distance) % count) for i in range(c...  6.93 us
    pallas_call x8, Pallas kernels, call(): pl.pallas_call(kernel, in_specs=[first] + [VMEM] * (len(args) - 1), out_s...  5.67 us
    ppermute x3, waiting for transfers between devices, from_all_domains(): return [block] + [lax.ppermute(block, 'dom', route) for route in routes]  3.89 us
    ppermute x3, starting transfers between devices, from_all_domains(): return [block] + [lax.ppermute(block, 'dom', route) for route in routes]  3.55 us
    unnamed x12, local copies, waits for them, and re-layouts  2.61 us
    slice x1, local copies, waits for them, and re-layouts, on_device(): two_a = along_bands(orbitals[:cut], 2)  1.25 us
    pallas_call x1, Pallas kernels, finish(): pl.pallas_call(finish_kernel, in_specs=[VMEM] * len(args), out_specs=pl.B...  1.17 us
  transfers between devices with their start and end apart: 12, of which 8 were waited for; matrix products, arithmetic and copies ran while one was open for 0% of the time, Pallas kernels for 14%

profile of v1, /device:TPU:0, one launch (start us, length us, event | category | flops | bytes accessed | tf_op | source)
XLA Modules:
  0.0 39.9 jit_solution(10396781183514438212)
XLA Ops:
  0.0 0.0 slice-start
  0.0 1.3 %slice.6 = bf16[48,6144]{1,0:T(8,128)(2,1)S(1)} slice(bf16[64,6144]{1,0:T(8,128)(2,1)} %own.3), slice={[0:48], [0:6144]} | slice | bytes 1179648 | tf_op jit(solution)/shard_map/slice | solution.py:309
  1.3 3.1 %collective-permute-start = (bf16[48,6144]{1,0:T(8,128)(2,1)S(1)}, bf16[48,6144]{1,0:T(8,128)(2,1)S(1)}, u32[]{:S(2)}, u32[]{:S(2)}) collective-permute-start(bf16[48,6144]{1,0:T(8,128)(2,1)S(1)} %slice.6), channel_id=1, source_target_pairs={{0,8},{4,12},{8,16},{12,20},{16,24},{20,28},{24,0},{28,4},{1,9},{5... | collective-permute-start | bytes 1769480 | tf_op jit(solution)/shard_map/ppermute | solution.py:42
  4.3 0.0 copy-start.2
  4.3 0.9 %copy-done.2 = f32[16,16,16]{2,1,0:T(8,128)S(1)} copy-done((f32[16,16,16]{2,1,0:T(8,128)S(1)}, f32[16,16,16]{2,1,0:T(8,128)}, u32[]{:S(2)}) %copy-start.2) | copy-done | bytes 16408
  5.2 0.0 copy-start
  5.2 0.0 slice-start.1
  5.2 0.1 turn.1.turned_ref
  5.4 0.0 slice-done
  5.4 1.0 %copy-done = bf16[64,6144]{1,0:T(8,128)(2,1)S(1)} copy-done((bf16[64,6144]{1,0:T(8,128)(2,1)S(1)}, bf16[64,6144]{1,0:T(8,128)(2,1)}, u32[]{:S(2)}) %copy-start) | copy-done | bytes 786456
  6.4 0.7 %slice-done.1 = s8[2097152]{0:T(1024)(128)(4,1)S(1)} async-done(((s8[6291456]{0:T(1024)(128)(4,1)}), s8[2097152]{0:T(1024)(128)(4,1)S(1)}, s32[]{:S(2)}) %slice-start.1) | async-done | bytes 2097176
  7.1 0.0 copy-start.3
  7.1 1.8 %project.1.refs_0_ = bf16[80,512]{1,0:T(8,128)(2,1)S(1)} custom-call(bf16[64,6144]{1,0:T(8,128)(2,1)S(1)} %copy-done, bf16[512,6144]{1,0:T(8,128)(2,1)S(1)} %bitcast.4, bf16[16,512]{1,0:T(8,128)(2,1)S(1)} %turn.1.turned_ref), custom_call_target="tpu_custom_call" | custom-call | tf_op jit(solution)/shard_map/project/pallas_call | solution.py:28
  8.9 2.5 %collective-permute-start.3 = (bf16[80,512]{1,0:T(8,128)(2,1)S(1)}, bf16[80,512]{1,0:T(8,128)(2,1)S(1)}, u32[]{:S(2)}, u32[]{:S(2)}) collective-permute-start(bf16[80,512]{1,0:T(8,128)(2,1)S(1)} %project.1.refs_0_), channel_id=1, source_target_pairs={{0,3},{1,2},{2,1},{3,0},{4,7},{5,6},{6,5},{7,4},{8,11},{9,10},{10,... | collective-permute-start | bytes 245768 | tf_op jit(solution)/shard_map/ppermute | solution.py:63
  11.4 0.5 %collective-permute-start.2 = (bf16[80,512]{1,0:T(8,128)(2,1)S(1)}, bf16[80,512]{1,0:T(8,128)(2,1)S(1)}, u32[]{:S(2)}, u32[]{:S(2)}) collective-permute-start(bf16[80,512]{1,0:T(8,128)(2,1)S(1)} %project.1.refs_0_), channel_id=1, source_target_pairs={{0,2},{1,3},{2,0},{3,1},{4,6},{5,7},{6,4},{7,5},{8,10},{9,11},{10,... | collective-permute-start | bytes 245768 | tf_op jit(solution)/shard_map/ppermute | solution.py:63
  11.9 0.5 %collective-permute-start.1 = (bf16[80,512]{1,0:T(8,128)(2,1)S(1)}, bf16[80,512]{1,0:T(8,128)(2,1)S(1)}, u32[]{:S(2)}, u32[]{:S(2)}) collective-permute-start(bf16[80,512]{1,0:T(8,128)(2,1)S(1)} %project.1.refs_0_), channel_id=1, source_target_pairs={{0,1},{1,0},{2,3},{3,2},{4,5},{5,4},{6,7},{7,6},{8,9},{9,8},{10,11... | collective-permute-start | bytes 245768 | tf_op jit(solution)/shard_map/ppermute | solution.py:63
  12.5 1.9 %collective-permute-done.3.refs_3_ = bf16[80,512]{1,0:T(8,128)(2,1)S(1)} collective-permute-done((bf16[80,512]{1,0:T(8,128)(2,1)S(1)}, bf16[80,512]{1,0:T(8,128)(2,1)S(1)}, u32[]{:S(2)}, u32[]{:S(2)}) %collective-permute-start.3) | collective-permute-done | bytes 81952 | tf_op jit(solution)/shard_map/ppermute | solution.py:63
  14.4 1.5 %collective-permute-done.2.refs_2_ = bf16[80,512]{1,0:T(8,128)(2,1)S(1)} collective-permute-done((bf16[80,512]{1,0:T(8,128)(2,1)S(1)}, bf16[80,512]{1,0:T(8,128)(2,1)S(1)}, u32[]{:S(2)}, u32[]{:S(2)}) %collective-permute-start.2) | collective-permute-done | bytes 81952 | tf_op jit(solution)/shard_map/ppermute | solution.py:63
  15.9 0.5 %collective-permute-done.1.refs_1_ = bf16[80,512]{1,0:T(8,128)(2,1)S(1)} collective-permute-done((bf16[80,512]{1,0:T(8,128)(2,1)S(1)}, bf16[80,512]{1,0:T(8,128)(2,1)S(1)}, u32[]{:S(2)}, u32[]{:S(2)}) %collective-permute-start.1) | collective-permute-done | bytes 81952 | tf_op jit(solution)/shard_map/ppermute | solution.py:63
  16.4 0.0 copy-done.3
  16.4 1.5 %couple.1 = (bf16[64,512]{1,0:T(8,128)(2,1)S(1)}, bf16[16,6144]{1,0:T(8,128)(2,1)S(1)}) custom-call(s32[4,32]{1,0:T(4,128)S(1)} %copy-done.3, bf16[80,512]{1,0:T(8,128)(2,1)S(1)} %project.1.refs_0_, bf16[80,512]{1,0:T(8,128)(2,1)S(1)} %collective-permute-done.1.refs_1_, bf16[80,512]{1,0:T(8,128)(2,1)S(1)} %collective-permute-done.2.refs_2_, ...), custom_call_target="tpu_custom_call" | custom-call | flops 2000000000 | tf_op jit(solution)/shard_map/couple/pallas_call | solution.py:28
  17.9 1.6 %collective-permute-start.5 = (bf16[64,512]{1,0:T(8,128)(2,1)S(1)}, bf16[64,512]{1,0:T(8,128)(2,1)S(1)}, u32[]{:S(2)}, u32[]{:S(2)}) collective-permute-start(bf16[64,512]{1,0:T(8,128)(2,1)S(1)} %get-tuple-element.13.even_ref.mine), channel_id=1, source_target_pairs={{0,8},{4,12},{8,16},{12,20},{16,24},{20,28},{24,0},{28,4},{1,9},{5... | collective-permute-start | bytes 196616 | tf_op jit(solution)/shard_map/ppermute | solution.py:42
  19.5 1.6 %collective-permute-start.4 = (bf16[16,6144]{1,0:T(8,128)(2,1)S(1)}, bf16[16,6144]{1,0:T(8,128)(2,1)S(1)}, u32[]{:S(2)}, u32[]{:S(2)}) collective-permute-start(bf16[16,6144]{1,0:T(8,128)(2,1)S(1)} %get-tuple-element.12), channel_id=1, source_target_pairs={{0,8},{4,12},{8,16},{12,20},{16,24},{20,28},{24,0},{28,4},{1,9},{5... | collective-permute-start | bytes 589832 | tf_op jit(solution)/shard_map/ppermute | solution.py:42
  21.1 3.6 %collective-permute-done.5.odd_ref = bf16[64,512]{1,0:T(8,128)(2,1)S(1)} collective-permute-done((bf16[64,512]{1,0:T(8,128)(2,1)S(1)}, bf16[64,512]{1,0:T(8,128)(2,1)S(1)}, u32[]{:S(2)}, u32[]{:S(2)}) %collective-permute-start.5) | collective-permute-done | bytes 65568 | tf_op jit(solution)/shard_map/ppermute | solution.py:42
  24.7 0.0 copy-start.1
  24.7 0.1 collective-permute-start.11
  24.8 0.1 collective-permute-start.10
  24.9 0.0 collective-permute-done.two_a.block_ref
  24.9 0.5 %collective-permute-start.7 = (bf16[48,6144]{1,0:T(8,128)(2,1)S(1)}, bf16[48,6144]{1,0:T(8,128)(2,1)S(1)}, u32[]{:S(2)}, u32[]{:S(2)}) collective-permute-start(bf16[48,6144]{1,0:T(8,128)(2,1)S(1)} %hold.1), channel_id=1, source_target_pairs={{0,4},{4,8},{8,12},{12,16},{16,20},{20,24},{24,28},{28,0},{1,5},{5... | collective-permute-start | bytes 1769480 | tf_op jit(solution)/shard_map/ppermute | solution.py:42
  25.5 2.1 %collective-permute-done.4.two_b = bf16[16,6144]{1,0:T(8,128)(2,1)S(1)} collective-permute-done((bf16[16,6144]{1,0:T(8,128)(2,1)S(1)}, bf16[16,6144]{1,0:T(8,128)(2,1)S(1)}, u32[]{:S(2)}, u32[]{:S(2)}) %collective-permute-start.4) | collective-permute-done | bytes 196640 | tf_op jit(solution)/shard_map/ppermute | solution.py:42
  27.6 0.1 choose.1
  27.6 0.1 collective-permute-start.9
  27.7 0.1 collective-permute-start.6
  27.8 2.5 %collective-permute-done.11.three = bf16[64,512]{1,0:T(8,128)(2,1)S(1)} collective-permute-done((bf16[64,512]{1,0:T(8,128)(2,1)S(1)}, bf16[64,512]{1,0:T(8,128)(2,1)S(1)}, u32[]{:S(2)}, u32[]{:S(2)}) %collective-permute-start.11) | collective-permute-done | bytes 65568 | tf_op jit(solution)/shard_map/ppermute | solution.py:42
  30.3 0.0 collective-permute-start.8
  30.3 0.0 collective-permute-done.10.one
  30.3 0.0 copy-done.1
  30.3 1.4 %apply.1.applied = f32[64,6144]{1,0:T(8,128)S(1)} custom-call(bf16[64,256]{1,0:T(8,128)(2,1)S(1)} %copy-done.1, bf16[64,512]{1,0:T(8,128)(2,1)S(1)} %get-tuple-element.13.even_ref.mine, bf16[64,512]{1,0:T(8,128)(2,1)S(1)} %collective-permute-done.10.one, bf16[64,512]{1,0:T(8,128)(2,1)S(1)} %get-tuple-element.18.two, ...), custom_call_target="tpu_custom_call" | custom-call | flops 6000000000 | tf_op jit(solution)/shard_map/apply/pallas_call | solution.py:28
  31.7 0.0 collective-permute-done.6.one_a
  31.7 4.8 %collective-permute-done.7.three_a = bf16[48,6144]{1,0:T(8,128)(2,1)S(1)} collective-permute-done((bf16[48,6144]{1,0:T(8,128)(2,1)S(1)}, bf16[48,6144]{1,0:T(8,128)(2,1)S(1)}, u32[]{:S(2)}, u32[]{:S(2)}) %collective-permute-start.7) | collective-permute-done | bytes 589856 | tf_op jit(solution)/shard_map/ppermute | solution.py:42
  36.6 0.6 %gather.1.partial_ref = f32[64,6144]{1,0:T(8,128)S(1)} custom-call(bf16[64,256]{1,0:T(8,128)(2,1)S(1)} %copy-done.1, bf16[64,6144]{1,0:T(8,128)(2,1)S(1)} %copy-done, bf16[32,6144]{1,0:T(8,128)(2,1)S(1)} %collective-permute-done.6.one_a, bf16[48,6144]{1,0:T(8,128)(2,1)S(1)} %collective-permute-done.two_a.block_ref, ...), custom_call_target="tpu_custom_call" | custom-call | tf_op jit(solution)/shard_map/gather/pallas_call | solution.py:28
  37.2 1.5 %collective-permute-done.9.three_b = bf16[16,6144]{1,0:T(8,128)(2,1)S(1)} collective-permute-done((bf16[16,6144]{1,0:T(8,128)(2,1)S(1)}, bf16[16,6144]{1,0:T(8,128)(2,1)S(1)}, u32[]{:S(2)}, u32[]{:S(2)}) %collective-permute-start.9) | collective-permute-done | bytes 196640 | tf_op jit(solution)/shard_map/ppermute | solution.py:42
  38.7 0.0 collective-permute-done.8.one_b
  38.7 1.2 %finish.1 = bf16[64,6144]{1,0:T(8,128)(2,1)} custom-call(bf16[64,256]{1,0:T(8,128)(2,1)S(1)} %copy-done.1, f32[64,6144]{1,0:T(8,128)S(1)} %gather.1.partial_ref, bf16[32,6144]{1,0:T(8,128)(2,1)S(1)} %collective-permute-done.8.one_b, bf16[16,6144]{1,0:T(8,128)(2,1)S(1)} %collective-permute-done.9.three_b, f32[64,6144]{1,0:T(8,128)S(1)} %apply.1.applied), custom_call_target="tpu_custom_call" | custom-call | tf_op jit(solution)/shard_map/finish/pallas_call | solution.py:290
  (4 shorter events, 0.1 us)
Async XLA Ops:
  0.0 5.4 %slice-start = ((s8[6291456]{0:T(1024)(128)(4,1)}), s8[4194304]{0:T(1024)(128)(4,1)S(1)}, s32[]{:S(2)}) async-start(s8[6291456]{0:T(1024)(128)(4,1)} %bitcast.2), calls=%async_computation | async-start | bytes 8388608
  1.3 23.6 %collective-permute-start = (bf16[48,6144]{1,0:T(8,128)(2,1)S(1)}, bf16[48,6144]{1,0:T(8,128)(2,1)S(1)}, u32[]{:S(2)}, u32[]{:S(2)}) collective-permute-start(bf16[48,6144]{1,0:T(8,128)(2,1)S(1)} %slice.6), channel_id=1, source_target_pairs={{0,8},{4,12},{8,16},{12,20},{16,24},{20,28},{24,0},{28,4},{1,9},{5... | collective-permute-start | bytes 1769480 | tf_op jit(solution)/shard_map/ppermute | solution.py:42
  4.3 0.9 %copy-start.2 = (f32[16,16,16]{2,1,0:T(8,128)S(1)}, f32[16,16,16]{2,1,0:T(8,128)}, u32[]{:S(2)}) copy-start(f32[16,16,16]{2,1,0:T(8,128)} %param.8) | copy-start | bytes 49156
  5.2 1.1 %copy-start = (bf16[64,6144]{1,0:T(8,128)(2,1)S(1)}, bf16[64,6144]{1,0:T(8,128)(2,1)}, u32[]{:S(2)}) copy-start(bf16[64,6144]{1,0:T(8,128)(2,1)} %own.3) | copy-start | bytes 2359300
  5.2 1.8 %slice-start.1 = ((s8[6291456]{0:T(1024)(128)(4,1)}), s8[2097152]{0:T(1024)(128)(4,1)S(1)}, s32[]{:S(2)}) async-start(s8[6291456]{0:T(1024)(128)(4,1)} %bitcast.2), calls=%async_computation.1 | async-start | bytes 4194304
  7.1 9.3 %copy-start.3 = (s32[4,32]{1,0:T(4,128)S(1)}, s32[4,32]{1,0:T(4,128)}, u32[]{:S(2)}) copy-start(s32[4,32]{1,0:T(4,128)} %slot_ref.1) | copy-start | bytes 1540
  8.9 5.5 %collective-permute-start.3 = (bf16[80,512]{1,0:T(8,128)(2,1)S(1)}, bf16[80,512]{1,0:T(8,128)(2,1)S(1)}, u32[]{:S(2)}, u32[]{:S(2)}) collective-permute-start(bf16[80,512]{1,0:T(8,128)(2,1)S(1)} %project.1.refs_0_), channel_id=1, source_target_pairs={{0,3},{1,2},{2,1},{3,0},{4,7},{5,6},{6,5},{7,4},{8,11},{9,10},{10,... | collective-permute-start | bytes 245768 | tf_op jit(solution)/shard_map/ppermute | solution.py:63
  11.4 4.5 %collective-permute-start.2 = (bf16[80,512]{1,0:T(8,128)(2,1)S(1)}, bf16[80,512]{1,0:T(8,128)(2,1)S(1)}, u32[]{:S(2)}, u32[]{:S(2)}) collective-permute-start(bf16[80,512]{1,0:T(8,128)(2,1)S(1)} %project.1.refs_0_), channel_id=1, source_target_pairs={{0,2},{1,3},{2,0},{3,1},{4,6},{5,7},{6,4},{7,5},{8,10},{9,11},{10,... | collective-permute-start | bytes 245768 | tf_op jit(solution)/shard_map/ppermute | solution.py:63
  11.9 4.4 %collective-permute-start.1 = (bf16[80,512]{1,0:T(8,128)(2,1)S(1)}, bf16[80,512]{1,0:T(8,128)(2,1)S(1)}, u32[]{:S(2)}, u32[]{:S(2)}) collective-permute-start(bf16[80,512]{1,0:T(8,128)(2,1)S(1)} %project.1.refs_0_), channel_id=1, source_target_pairs={{0,1},{1,0},{2,3},{3,2},{4,5},{5,4},{6,7},{7,6},{8,9},{9,8},{10,11... | collective-permute-start | bytes 245768 | tf_op jit(solution)/shard_map/ppermute | solution.py:63
  17.9 6.8 %collective-permute-start.5 = (bf16[64,512]{1,0:T(8,128)(2,1)S(1)}, bf16[64,512]{1,0:T(8,128)(2,1)S(1)}, u32[]{:S(2)}, u32[]{:S(2)}) collective-permute-start(bf16[64,512]{1,0:T(8,128)(2,1)S(1)} %get-tuple-element.13.even_ref.mine), channel_id=1, source_target_pairs={{0,8},{4,12},{8,16},{12,20},{16,24},{20,28},{24,0},{28,4},{1,9},{5... | collective-permute-start | bytes 196616 | tf_op jit(solution)/shard_map/ppermute | solution.py:42
  19.5 8.0 %collective-permute-start.4 = (bf16[16,6144]{1,0:T(8,128)(2,1)S(1)}, bf16[16,6144]{1,0:T(8,128)(2,1)S(1)}, u32[]{:S(2)}, u32[]{:S(2)}) collective-permute-start(bf16[16,6144]{1,0:T(8,128)(2,1)S(1)} %get-tuple-element.12), channel_id=1, source_target_pairs={{0,8},{4,12},{8,16},{12,20},{16,24},{20,28},{24,0},{28,4},{1,9},{5... | collective-permute-start | bytes 589832 | tf_op jit(solution)/shard_map/ppermute | solution.py:42
  24.7 5.6 %copy-start.1 = (bf16[64,256]{1,0:T(8,128)(2,1)S(1)}, bf16[64,256]{1,0:T(8,128)(2,1)}, u32[]{:S(2)}) copy-start(bf16[64,256]{1,0:T(8,128)(2,1)} %rot_ref.5) | copy-start | bytes 98308
  24.7 5.5 %collective-permute-start.11 = (bf16[64,512]{1,0:T(8,128)(2,1)S(1)}, bf16[64,512]{1,0:T(8,128)(2,1)S(1)}, u32[]{:S(2)}, u32[]{:S(2)}) collective-permute-start(bf16[64,512]{1,0:T(8,128)(2,1)S(1)} %get-tuple-element.18.two), channel_id=1, source_target_pairs={{0,4},{4,8},{8,12},{12,16},{16,20},{20,24},{24,28},{28,0},{1,5},{5... | collective-permute-start | bytes 196616 | tf_op jit(solution)/shard_map/ppermute | solution.py:42
  24.8 5.5 %collective-permute-start.10 = (bf16[64,512]{1,0:T(8,128)(2,1)S(1)}, bf16[64,512]{1,0:T(8,128)(2,1)S(1)}, u32[]{:S(2)}, u32[]{:S(2)}) collective-permute-start(bf16[64,512]{1,0:T(8,128)(2,1)S(1)} %get-tuple-element.14.after_ref), channel_id=1, source_target_pairs={{0,4},{4,0},{8,12},{12,8},{16,20},{20,16},{24,28},{28,24},{1,5},{5... | collective-permute-start | bytes 196616 | tf_op jit(solution)/shard_map/ppermute | solution.py:47
  24.9 11.7 %collective-permute-start.7 = (bf16[48,6144]{1,0:T(8,128)(2,1)S(1)}, bf16[48,6144]{1,0:T(8,128)(2,1)S(1)}, u32[]{:S(2)}, u32[]{:S(2)}) collective-permute-start(bf16[48,6144]{1,0:T(8,128)(2,1)S(1)} %hold.1), channel_id=1, source_target_pairs={{0,4},{4,8},{8,12},{12,16},{16,20},{20,24},{24,28},{28,0},{1,5},{5... | collective-permute-start | bytes 1769480 | tf_op jit(solution)/shard_map/ppermute | solution.py:42
  27.6 11.1 %collective-permute-start.9 = (bf16[16,6144]{1,0:T(8,128)(2,1)S(1)}, bf16[16,6144]{1,0:T(8,128)(2,1)S(1)}, u32[]{:S(2)}, u32[]{:S(2)}) collective-permute-start(bf16[16,6144]{1,0:T(8,128)(2,1)S(1)} %get-tuple-element.17), channel_id=1, source_target_pairs={{0,4},{4,8},{8,12},{12,16},{16,20},{20,24},{24,28},{28,0},{1,5},{5... | collective-permute-start | bytes 589832 | tf_op jit(solution)/shard_map/ppermute | solution.py:42
  27.7 4.0 %collective-permute-start.6 = (bf16[32,6144]{1,0:T(8,128)(2,1)S(1)}, bf16[32,6144]{1,0:T(8,128)(2,1)S(1)}, u32[]{:S(2)}, u32[]{:S(2)}) collective-permute-start(bf16[32,6144]{1,0:T(8,128)(2,1)S(1)} %get-tuple-element.15), channel_id=1, source_target_pairs={{0,4},{4,0},{8,12},{12,8},{16,20},{20,16},{24,28},{28,24},{1,5},{5... | collective-permute-start | bytes 1179656 | tf_op jit(solution)/shard_map/ppermute | solution.py:47
  30.3 8.4 %collective-permute-start.8 = (bf16[32,6144]{1,0:T(8,128)(2,1)S(1)}, bf16[32,6144]{1,0:T(8,128)(2,1)S(1)}, u32[]{:S(2)}, u32[]{:S(2)}) collective-permute-start(bf16[32,6144]{1,0:T(8,128)(2,1)S(1)} %get-tuple-element.16), channel_id=1, source_target_pairs={{0,4},{4,0},{8,12},{12,8},{16,20},{20,16},{24,28},{28,24},{1,5},{5... | collective-permute-start | bytes 1179656 | tf_op jit(solution)/shard_map/ppermute | solution.py:47
